TPU v7x, 512 devices: a whole 4x4x16 slice. The times are simulated.
512 devices in a mesh: dp: 16 (over y, x_hi, core), ctx: 32 (over z, x_lo).
Axes of the slice: x: 4 (x_hi: 2, x_lo: 2; x = x_hi * 2 + x_lo), y: 4, z: 16, core: 2. Of those that a mesh axis runs over, the one named last changes fastest.
Arguments:
- out_gate: bfloat16 [16, 8192, 512], P('dp', 'ctx'), may hold values from -6 to 6
- key_gate: bfloat16 [16, 8192, 512], P('dp', 'ctx'), may hold values from -6 to 6
- value_input: bfloat16 [16, 8192, 512], P('dp', 'ctx'), may hold values from -6 to 6
- filter_taps: bfloat16 [8192, 512], P('ctx'), may hold values from -2 to 2
- cotangent: bfloat16 [16, 8192, 512], P('dp', 'ctx'), may hold values from -6 to 6
- block_live: int32 [16, 128], P('dp', 'ctx'), may hold values 0 or 1
Outputs:
- grad_out_gate: bfloat16 [16, 8192, 512], P('dp', 'ctx')
- grad_key_gate: bfloat16 [16, 8192, 512], P('dp', 'ctx')
- grad_value: bfloat16 [16, 8192, 512], P('dp', 'ctx')
- grad_taps: bfloat16 [8192, 512], P('ctx')
Inputs may be any that keep to these rules, and one draw needn't show every extreme that they name: `block_live`: 1 where a block of 64 tokens holds sequence data, 0 where it is padding.
All inputs are finite; a program needn't handle non-finite values.
Results may differ from a plain program's by a relative error of at most 0.027.
Values may be sent and summed in bfloat16 or wider, within the bound.
A program may use at most 64 MiB of HBM per device.

v0:
```python
import math
import jax
import jax.numpy as jnp
from jax import lax
from jax.sharding import PartitionSpec as P

QLEN = 64
PROWS = 4
TWO_PI = 2.0 * math.pi


def angle_table(row_count, col_count, row_start, col_start, period_len, direction):
    row_ids = jnp.arange(row_count, dtype=jnp.int32)[:, None] + row_start
    col_ids = jnp.arange(col_count, dtype=jnp.int32)[None, :] + col_start
    phases = (row_ids * col_ids % period_len).astype(jnp.float32)
    return direction * TWO_PI * phases / period_len


def factor_tables(angles):
    return (jnp.cos(angles).astype(jnp.bfloat16), jnp.sin(angles).astype(jnp.bfloat16))


def rotate_pair(real_part, imag_part, angles):
    turn_cos = jnp.cos(angles)[None, :, :, None]
    turn_sin = jnp.sin(angles)[None, :, :, None]
    return (
        real_part * turn_cos - imag_part * turn_sin,
        real_part * turn_sin + imag_part * turn_cos,
    )


def forward_transform(signals):
    ctx_count = lax.axis_size("ctx")
    ctx_place = lax.axis_index("ctx")
    full_rows = 2 * signals.shape[1] * ctx_count
    col_count = signals.shape[2]
    col_share = col_count // ctx_count
    total_len = full_rows * col_count
    cos_rows, sin_rows = factor_tables(
        angle_table(full_rows, full_rows // 2, 0, 0, full_rows, -1.0)
    )
    twist_angles = angle_table(full_rows, col_share, 0, ctx_place * col_share, total_len, -1.0)
    cos_cols, sin_cols = factor_tables(angle_table(col_count, col_count, 0, 0, col_count, -1.0))
    spread = lax.all_to_all(signals, "ctx", split_axis=2, concat_axis=1, tiled=True)
    real_part = jnp.einsum("kp,spac->skac", cos_rows, spread, preferred_element_type=jnp.float32)
    imag_part = jnp.einsum("kp,spac->skac", sin_rows, spread, preferred_element_type=jnp.float32)
    real_part, imag_part = rotate_pair(real_part, imag_part, twist_angles)
    packed = jnp.stack([real_part, imag_part]).astype(jnp.bfloat16)
    regrouped = lax.all_to_all(packed, "ctx", split_axis=2, concat_axis=3, tiled=True)
    real_in = regrouped[0]
    imag_in = regrouped[1]
    real_out = jnp.einsum(
        "saqc,qk->sakc", real_in, cos_cols, preferred_element_type=jnp.float32
    ) - jnp.einsum("saqc,qk->sakc", imag_in, sin_cols, preferred_element_type=jnp.float32)
    imag_out = jnp.einsum(
        "saqc,qk->sakc", real_in, sin_cols, preferred_element_type=jnp.float32
    ) + jnp.einsum("saqc,qk->sakc", imag_in, cos_cols, preferred_element_type=jnp.float32)
    return jnp.stack([real_out, imag_out]).astype(jnp.bfloat16)


def inverse_transform(spectra):
    ctx_count = lax.axis_size("ctx")
    ctx_place = lax.axis_index("ctx")
    row_share = spectra.shape[2]
    col_count = spectra.shape[3]
    full_rows = row_share * ctx_count
    total_len = full_rows * col_count
    cos_cols, sin_cols = factor_tables(angle_table(col_count, col_count, 0, 0, col_count, 1.0))
    twist_angles = angle_table(row_share, col_count, ctx_place * row_share, 0, total_len, 1.0)
    cos_back, sin_back = factor_tables(angle_table(full_rows // 2, full_rows, 0, 0, full_rows, 1.0))
    real_in = spectra[0]
    imag_in = spectra[1]
    real_part = jnp.einsum(
        "sakc,kq->saqc", real_in, cos_cols, preferred_element_type=jnp.float32
    ) - jnp.einsum("sakc,kq->saqc", imag_in, sin_cols, preferred_element_type=jnp.float32)
    imag_part = jnp.einsum(
        "sakc,kq->saqc", real_in, sin_cols, preferred_element_type=jnp.float32
    ) + jnp.einsum("sakc,kq->saqc", imag_in, cos_cols, preferred_element_type=jnp.float32)
    real_part, imag_part = rotate_pair(real_part, imag_part, twist_angles)
    twisted = jnp.stack([real_part, imag_part]).astype(jnp.bfloat16)
    gathered = lax.all_to_all(twisted, "ctx", split_axis=3, concat_axis=2, tiled=True)
    signal = jnp.einsum(
        "pk,skac->spac", cos_back, gathered[0], preferred_element_type=jnp.float32
    ) - jnp.einsum("pk,skac->spac", sin_back, gathered[1], preferred_element_type=jnp.float32)
    spread = (signal * (1.0 / total_len)).astype(jnp.bfloat16)
    return lax.all_to_all(spread, "ctx", split_axis=1, concat_axis=2, tiled=True)


def spectrum_product(left_spec, right_spec, conjugate):
    left_real = left_spec[0].astype(jnp.float32)
    left_imag = left_spec[1].astype(jnp.float32)
    right_real = right_spec[0].astype(jnp.float32)
    right_imag = right_spec[1].astype(jnp.float32)
    if conjugate:
        real_out = left_real * right_real + left_imag * right_imag
        imag_out = left_imag * right_real - left_real * right_imag
    else:
        real_out = left_real * right_real - left_imag * right_imag
        imag_out = left_real * right_imag + left_imag * right_real
    return jnp.stack([real_out, imag_out]).astype(jnp.bfloat16)


def local(out_gate, key_gate, value_input, filter_taps, cotangent, block_live):
    tok_count = key_gate.shape[1]
    chan_count = key_gate.shape[2]
    block_count = block_live.shape[1]
    grid_shape = (PROWS, QLEN, chan_count)
    live_rows = block_live[0].astype(jnp.float32)[:, None, None]

    def masked(values):
        return (
            values.reshape(block_count, tok_count // block_count, chan_count) * live_rows
        ).reshape(tok_count, chan_count)

    key_wide = key_gate[0].astype(jnp.float32)
    value_wide = value_input[0].astype(jnp.float32)
    cot_wide = cotangent[0].astype(jnp.float32)
    gated_input = masked(key_wide * value_wide).astype(jnp.bfloat16).reshape(grid_shape)
    back_signal = (
        (cot_wide * out_gate[0].astype(jnp.float32)).astype(jnp.bfloat16).reshape(grid_shape)
    )
    taps_grid = filter_taps.reshape(grid_shape)
    filter_spec = None
    extra_signals = [taps_grid]
    first_spectra = forward_transform(jnp.stack([gated_input] + extra_signals))
    filter_spec = first_spectra[:, 1]
    forward_spec = first_spectra[:, 0]
    conv_out = inverse_transform(spectrum_product(forward_spec, filter_spec, False)[:, None])[0]
    backward_spec = forward_transform(back_signal[None])[:, 0]
    restored = inverse_transform(
        jnp.stack(
            [
                spectrum_product(backward_spec, filter_spec, True),
                spectrum_product(backward_spec, forward_spec, True),
            ],
            axis=1,
        )
    )
    grad_conv = restored[0]
    taps_seq = restored[1]
    conv_flat = conv_out.reshape(tok_count, chan_count).astype(jnp.float32)
    grad_gate = (cot_wide * conv_flat).astype(jnp.bfloat16)
    grad_flat = grad_conv.reshape(tok_count, chan_count).astype(jnp.float32)
    grad_key = masked(grad_flat * value_wide).astype(jnp.bfloat16)
    grad_value = masked(grad_flat * key_wide).astype(jnp.bfloat16)
    scale_factor = 1.0 / math.sqrt(lax.axis_size("dp") * tok_count * lax.axis_size("ctx"))
    taps_sum = lax.psum(
        taps_seq.reshape(tok_count, chan_count).astype(jnp.float32).astype(jnp.bfloat16), "dp"
    ).astype(jnp.float32)
    grad_taps = (taps_sum * scale_factor).astype(jnp.bfloat16)
    return (grad_gate[None], grad_key[None], grad_value[None], grad_taps)


def solution(mesh):
    return jax.shard_map(
        local,
        mesh=mesh,
        in_specs=(
            P("dp", "ctx", None),
            P("dp", "ctx", None),
            P("dp", "ctx", None),
            P("ctx", None),
            P("dp", "ctx", None),
            P("dp", "ctx"),
        ),
        out_specs=(
            P("dp", "ctx", None),
            P("dp", "ctx", None),
            P("dp", "ctx", None),
            P("ctx", None),
        ),
        check_vma=False,
    )
```

profile of v0, /device:TPU:1, one launch (start us, length us, event | category | flops | bytes accessed | tf_op | source)
XLA Modules:
  0.0 641.4 jit_solution(15273747222807358933)
XLA Ops:
  7.2 1.6 fusion.64
  8.9 0.9 copy.209
  9.8 17.0 %all-to-all-start.4 = ((bf16[1,4,64,512]{3,1,0,2:T(4,128)(2,1)}), bf16[1,4,64,512]{3,1,0,2:T(4,128)(2,1)S(1)}, u32[]{:S(2)}, u32[]{:S(2)}) async-start(bf16[1,4,64,512]{3,1,0,2:T(4,128)(2,1)} %copy.209), calls=%async_computation.4 | async-start | bytes 524288 | tf_op jit(solution)/shard_map/all_to_all | solution.py:44
  27.6 1.2 copy.191
  28.8 18.5 %all-to-all-done.4 = bf16[1,4,64,512]{3,1,0,2:T(4,128)(2,1)S(1)} async-done(((bf16[1,4,64,512]{3,1,0,2:T(4,128)(2,1)}), bf16[1,4,64,512]{3,1,0,2:T(4,128)(2,1)S(1)}, u32[]{:S(2)}, u32[]{:S(2)}) %all-to-all-start.4) | async-done | bytes 262176 | tf_op jit(solution)/shard_map/all_to_all | solution.py:44
  47.3 3.9 all-to-all-start
  52.6 0.9 fusion.51
  53.6 2.1 copy.213
  55.7 26.1 %all-to-all-done = bf16[2,4,64,512]{3,1,0,2:T(4,128)(2,1)S(1)} async-done(((bf16[2,4,64,512]{3,1,0,2:T(4,128)(2,1)}), bf16[2,4,64,512]{3,1,0,2:T(4,128)(2,1)S(1)}, u32[]{:S(2)}, u32[]{:S(2)}) %all-to-all-start) | async-done | bytes 524320 | tf_op jit(solution)/shard_map/all_to_all | solution.py:44
  81.8 4.6 all-to-all-start.5
  87.3 0.9 fusion.82
  88.2 1.1 fusion.39
  89.6 4.1 copy.196
  93.7 44.4 %all-to-all-done.5 = bf16[2,1,256,2,512]{4,3,1,0,2:T(2,128)(2,1)S(1)} async-done(((bf16[2,1,256,2,512]{4,3,1,0,2:T(2,128)(2,1)}), bf16[2,1,256,2,512]{4,3,1,0,2:T(2,128)(2,1)S(1)}, u32[]{:S(2)}, u32[]{:S(2)}) %all-to-all-start.5) | async-done | bytes 1048608 | tf_op jit(solution)/shard_map/all_to_all | solution.py:49
  138.1 6.8 %all-to-all-start.1 = ((bf16[2,2,256,2,512]{4,3,1,0,2:T(2,128)(2,1)}), bf16[2,2,256,2,512]{4,3,1,0,2:T(2,128)(2,1)S(1)}, u32[]{:S(2)}, u32[]{:S(2)}) async-start(bf16[2,2,256,2,512]{4,3,1,0,2:T(2,128)(2,1)} %copy.196), calls=%async_computation.1 | async-start | bytes 4194304 | tf_op jit(solution)/shard_map/all_to_all | solution.py:49
  145.2 0.9 fusion.228
  146.9 2.4 copy.216
  149.2 1.2 reshape.608
  150.9 1.4 fusion.18
  152.3 1.4 fusion.103
  153.7 86.9 %all-to-all-done.1 = bf16[2,2,256,2,512]{4,3,1,0,2:T(2,128)(2,1)S(1)} async-done(((bf16[2,2,256,2,512]{4,3,1,0,2:T(2,128)(2,1)}), bf16[2,2,256,2,512]{4,3,1,0,2:T(2,128)(2,1)S(1)}, u32[]{:S(2)}, u32[]{:S(2)}) %all-to-all-start.1) | async-done | bytes 2097184 | tf_op jit(solution)/shard_map/all_to_all | solution.py:49
  241.3 1.2 fusion.227
  242.5 1.1 copy.198
  244.0 1.9 fusion.111
  247.1 2.1 copy.199
  249.2 1.5 squeeze.13
  250.7 2.1 fusion.9
  254.5 1.1 fusion.33
  257.5 1.6 copy.200
  259.0 7.4 %all-to-all-start.2 = ((bf16[2,1,8,64,512]{4,2,1,0,3:T(8,128)(2,1)}), bf16[2,1,8,64,512]{4,2,1,0,3:T(8,128)(2,1)S(1)}, u32[]{:S(2)}, u32[]{:S(2)}) async-start(bf16[2,1,8,64,512]{4,2,1,0,3:T(8,128)(2,1)} %copy.200), calls=%async_computation.2 | async-start | bytes 2097152 | tf_op jit(solution)/shard_map/all_to_all | solution.py:81
  268.3 0.9 fusion.41
  269.4 2.5 copy.217
  271.9 47.3 %all-to-all-done.2 = bf16[2,1,8,64,512]{4,2,1,0,3:T(8,128)(2,1)S(1)} async-done(((bf16[2,1,8,64,512]{4,2,1,0,3:T(8,128)(2,1)}), bf16[2,1,8,64,512]{4,2,1,0,3:T(8,128)(2,1)S(1)}, u32[]{:S(2)}, u32[]{:S(2)}) %all-to-all-start.2) | async-done | bytes 1048608 | tf_op jit(solution)/shard_map/all_to_all | solution.py:81
  319.2 5.9 all-to-all-start.6
  326.0 0.8 fusion.25
  326.9 0.9 copy.206
  327.7 93.3 %all-to-all-done.6 = bf16[2,2,8,64,512]{4,2,1,0,3:T(8,128)(2,1)S(1)} async-done(((bf16[2,2,8,64,512]{4,2,1,0,3:T(8,128)(2,1)}), bf16[2,2,8,64,512]{4,2,1,0,3:T(8,128)(2,1)S(1)}, u32[]{:S(2)}, u32[]{:S(2)}) %all-to-all-start.6) | async-done | bytes 2097184 | tf_op jit(solution)/shard_map/all_to_all | solution.py:81
  421.0 7.3 %all-to-all-start.3 = ((bf16[1,128,2,512]{3,2,0,1:T(2,128)(2,1)}), bf16[1,128,2,512]{3,2,0,1:T(2,128)(2,1)S(1)}, u32[]{:S(2)}, u32[]{:S(2)}) async-start(bf16[1,128,2,512]{3,2,0,1:T(2,128)(2,1)} %copy.206), calls=%async_computation.3 | async-start | bytes 524288 | tf_op jit(solution)/shard_map/all_to_all | solution.py:86
  428.8 0.9 fusion.43
  429.7 1.0 fusion.22
  430.7 1.1 copy.223
  431.8 16.0 %all-to-all-done.3 = bf16[1,128,2,512]{3,2,0,1:T(2,128)(2,1)S(1)} async-done(((bf16[1,128,2,512]{3,2,0,1:T(2,128)(2,1)}), bf16[1,128,2,512]{3,2,0,1:T(2,128)(2,1)S(1)}, u32[]{:S(2)}, u32[]{:S(2)}) %all-to-all-start.3) | async-done | bytes 262176 | tf_op jit(solution)/shard_map/all_to_all | solution.py:86
  447.8 4.8 all-to-all-start.7
  455.3 26.7 %all-to-all-done.7 = bf16[2,128,2,512]{3,2,0,1:T(2,128)(2,1)S(1)} async-done(((bf16[2,128,2,512]{3,2,0,1:T(2,128)(2,1)}), bf16[2,128,2,512]{3,2,0,1:T(2,128)(2,1)S(1)}, u32[]{:S(2)}, u32[]{:S(2)}) %all-to-all-start.7) | async-done | bytes 524320 | tf_op jit(solution)/shard_map/all_to_all | solution.py:86
  483.2 0.8 reshape_squeeze.2
  484.0 2.6 fusion.58
  488.1 144.7 %all-reduce.2.cloned.1.call-done = bf16[256,512]{1,0:T(8,128)(2,1)} async-done(((bf16[256,512]{1,0:T(8,128)(2,1)}), bf16[256,512]{1,0:T(8,128)(2,1)}) %all-reduce.2.cloned.1.call-update) | async-done | bytes 262160 | tf_op jit(solution)/shard_map/psum | solution.py:147
  632.9 1.7 multiply_convert_fusion
  (76 shorter events, 19.2 us)
Async XLA Ops:
  7.2 19.6 %copy-start.6 = (bf16[1,256,512]{2,1,0:T(8,128)(2,1)S(1)}, bf16[1,256,512]{2,1,0:T(8,128)(2,1)}, u32[]{:S(2)}) copy-start(bf16[1,256,512]{2,1,0:T(8,128)(2,1)} %param.7) | copy-start | bytes 786436
  7.2 19.6 %copy-start.7 = (bf16[1,256,512]{2,1,0:T(8,128)(2,1)S(1)}, bf16[1,256,512]{2,1,0:T(8,128)(2,1)}, u32[]{:S(2)}) copy-start(bf16[1,256,512]{2,1,0:T(8,128)(2,1)} %param.8) | copy-start | bytes 786436
  8.8 18.6 %copy-start.10 = (s32[1,4]{1,0:T(1,128)S(1)}, s32[1,4]{1,0:T(1,128)}, u32[]{:S(2)}) copy-start(s32[1,4]{1,0:T(1,128)} %param.11) | copy-start | bytes 52
  8.9 18.6 %copy-start.9 = (bf16[256,512]{1,0:T(8,128)(2,1)S(1)}, bf16[256,512]{1,0:T(8,128)(2,1)}, u32[]{:S(2)}) copy-start(bf16[256,512]{1,0:T(8,128)(2,1)} %param.9) | copy-start | bytes 786436
  9.8 37.5 %all-to-all-start.4 = ((bf16[1,4,64,512]{3,1,0,2:T(4,128)(2,1)}), bf16[1,4,64,512]{3,1,0,2:T(4,128)(2,1)S(1)}, u32[]{:S(2)}, u32[]{:S(2)}) async-start(bf16[1,4,64,512]{3,1,0,2:T(4,128)(2,1)} %copy.209), calls=%async_computation.4 | async-start | bytes 524288 | tf_op jit(solution)/shard_map/all_to_all | solution.py:44
  47.3 34.5 %all-to-all-start = ((bf16[2,4,64,512]{3,1,0,2:T(4,128)(2,1)}), bf16[2,4,64,512]{3,1,0,2:T(4,128)(2,1)S(1)}, u32[]{:S(2)}, u32[]{:S(2)}) async-start(bf16[2,4,64,512]{3,1,0,2:T(4,128)(2,1)} %copy.191), calls=%async_computation | async-start | bytes 1048576 | tf_op jit(solution)/shard_map/all_to_all | solution.py:44
  81.8 56.3 %all-to-all-start.5 = ((bf16[2,1,256,2,512]{4,3,1,0,2:T(2,128)(2,1)}), bf16[2,1,256,2,512]{4,3,1,0,2:T(2,128)(2,1)S(1)}, u32[]{:S(2)}, u32[]{:S(2)}) async-start(bf16[2,1,256,2,512]{4,3,1,0,2:T(2,128)(2,1)} %copy.213), calls=%async_computation.5 | async-start | bytes 2097152 | tf_op jit(solution)/shard_map/all_to_all | solution.py:49
  138.1 102.5 %all-to-all-start.1 = ((bf16[2,2,256,2,512]{4,3,1,0,2:T(2,128)(2,1)}), bf16[2,2,256,2,512]{4,3,1,0,2:T(2,128)(2,1)S(1)}, u32[]{:S(2)}, u32[]{:S(2)}) async-start(bf16[2,2,256,2,512]{4,3,1,0,2:T(2,128)(2,1)} %copy.196), calls=%async_computation.1 | async-start | bytes 4194304 | tf_op jit(solution)/shard_map/all_to_all | solution.py:49
  150.5 1.8 copy-start.1
  245.9 1.2 copy-start
  252.8 1.0 copy-start.2
  252.8 1.4 copy-start.3
  252.8 1.7 copy-start.4
  259.0 60.2 %all-to-all-start.2 = ((bf16[2,1,8,64,512]{4,2,1,0,3:T(8,128)(2,1)}), bf16[2,1,8,64,512]{4,2,1,0,3:T(8,128)(2,1)S(1)}, u32[]{:S(2)}, u32[]{:S(2)}) async-start(bf16[2,1,8,64,512]{4,2,1,0,3:T(8,128)(2,1)} %copy.200), calls=%async_computation.2 | async-start | bytes 2097152 | tf_op jit(solution)/shard_map/all_to_all | solution.py:81
  319.2 101.8 %all-to-all-start.6 = ((bf16[2,2,8,64,512]{4,2,1,0,3:T(8,128)(2,1)}), bf16[2,2,8,64,512]{4,2,1,0,3:T(8,128)(2,1)S(1)}, u32[]{:S(2)}, u32[]{:S(2)}) async-start(bf16[2,2,8,64,512]{4,2,1,0,3:T(8,128)(2,1)} %copy.217), calls=%async_computation.6 | async-start | bytes 4194304 | tf_op jit(solution)/shard_map/all_to_all | solution.py:81
  421.0 26.8 %all-to-all-start.3 = ((bf16[1,128,2,512]{3,2,0,1:T(2,128)(2,1)}), bf16[1,128,2,512]{3,2,0,1:T(2,128)(2,1)S(1)}, u32[]{:S(2)}, u32[]{:S(2)}) async-start(bf16[1,128,2,512]{3,2,0,1:T(2,128)(2,1)} %copy.206), calls=%async_computation.3 | async-start | bytes 524288 | tf_op jit(solution)/shard_map/all_to_all | solution.py:86
  430.7 23.3 %copy-start.5 = (bf16[1,256,512]{2,1,0:T(8,128)(2,1)S(1)}, bf16[1,256,512]{2,1,0:T(8,128)(2,1)}, u32[]{:S(2)}) copy-start(bf16[1,256,512]{2,1,0:T(8,128)(2,1)} %param.10) | copy-start | bytes 786436
  447.8 34.2 %all-to-all-start.7 = ((bf16[2,128,2,512]{3,2,0,1:T(2,128)(2,1)}), bf16[2,128,2,512]{3,2,0,1:T(2,128)(2,1)S(1)}, u32[]{:S(2)}, u32[]{:S(2)}) async-start(bf16[2,128,2,512]{3,2,0,1:T(2,128)(2,1)} %copy.223), calls=%async_computation.7 | async-start | bytes 1048576 | tf_op jit(solution)/shard_map/all_to_all | solution.py:86
  452.6 180.2 %all-reduce.2.cloned.1.call-start = ((), (), s32[]{:S(2)}) async-start(), calls=%async_computation.8 | async-start | bytes 524288 | tf_op jit(solution)/shard_map/psum | solution.py:147
  482.3 1.7 copy-start.8
Sparse Core Ops, SparseCore 0:
  484.1 148.6 all-reduce.1
where the time goes:
time: 642 us; the launch traced here: 641 us
  waiting for transfers between devices  504 us (79%)
  starting transfers between devices  58 us (9%)
  local copies, waits for them, and re-layouts  35.6 us (6%)
  matrix products  20.7 us (3%)
  between operations  14.6 us (2%)
  other arithmetic  8.59 us (1%)
    psum x1, waiting for transfers between devices, local(): lax.psum(taps_seq.reshape(tok_count, chan_count).astype(jnp.float32).asty...  145 us
    all_to_all x2, waiting for transfers between devices, inverse_transform(): lax.all_to_all(twisted, 'ctx', split_axis=3, concat_axis=2, tiled=True)  141 us
    all_to_all x2, waiting for transfers between devices, forward_transform(): lax.all_to_all(packed, 'ctx', split_axis=2, concat_axis=3, tiled=True)  131 us
    all_to_all x2, waiting for transfers between devices, forward_transform(): lax.all_to_all(signals, 'ctx', split_axis=2, concat_axis=1, tiled=True)  44.6 us
    all_to_all x2, waiting for transfers between devices, inverse_transform(): lax.all_to_all(spread, 'ctx', split_axis=1, concat_axis=2, tiled=True)  42.7 us
    all_to_all x2, starting transfers between devices, forward_transform(): lax.all_to_all(signals, 'ctx', split_axis=2, concat_axis=1, tiled=True)  20.9 us
    all_to_all x2, starting transfers between devices, inverse_transform(): lax.all_to_all(twisted, 'ctx', split_axis=3, concat_axis=2, tiled=True)  13.3 us
  transfers between devices with their start and end apart: 9, of which 9 were waited for; matrix products, arithmetic and copies ran while one was open for 6% of the time, Pallas kernels for 0%

commit v1 on v0

--- a/solution.py
+++ b/solution.py
@@ -144,8 +144,9 @@
     grad_key = masked(grad_flat * value_wide).astype(jnp.bfloat16)
     grad_value = masked(grad_flat * key_wide).astype(jnp.bfloat16)
     scale_factor = 1.0 / math.sqrt(lax.axis_size("dp") * tok_count * lax.axis_size("ctx"))
-    taps_sum = lax.psum(
-        taps_seq.reshape(tok_count, chan_count).astype(jnp.float32).astype(jnp.bfloat16), "dp"
+    _feed_ranges = lambda my_data: jnp.sum(lax.all_gather(my_data, "dp"), axis=0)
+    taps_sum = _feed_ranges(
+        taps_seq.reshape(tok_count, chan_count).astype(jnp.float32).astype(jnp.bfloat16)
     ).astype(jnp.float32)
     grad_taps = (taps_sum * scale_factor).astype(jnp.bfloat16)
     return (grad_gate[None], grad_key[None], grad_value[None], grad_taps)

time: 642 us -> 514 us (0.80)
  waiting for transfers between devices: 504 us -> 196 us
  blocking collectives: 0 us -> 199 us
  starting transfers between devices: 58 us -> 38.4 us
    all_to_all x0 -> x3, blocking collectives: none -> 199 us  [the longest x2 162 us: inverse_transform(): lax.all_to_all(twisted, 'ctx', split_axis=3, concat_axis=2, tiled=True)]
    psum x1 -> x0, waiting for transfers between devices: 145 us -> none  [local(): lax.psum(taps_seq.reshape(tok_count, chan_count).astype(jnp.float32).asty...]
    all_to_all x2 -> x0, waiting for transfers between devices: 141 us -> none  [inverse_transform(): lax.all_to_all(twisted, 'ctx', split_axis=3, concat_axis=2, tiled=True)]
    all_to_all x2 -> x1, waiting for transfers between devices: 42.7 us -> 19.7 us  [inverse_transform(): lax.all_to_all(spread, 'ctx', split_axis=1, concat_axis=2, tiled=True)]
    all_to_all x2 -> x0, starting transfers between devices: 13.3 us -> none  [inverse_transform(): lax.all_to_all(twisted, 'ctx', split_axis=3, concat_axis=2, tiled=True)]
  transfers between devices with their start and end apart: 9 -> 6, of which waited for: 9 -> 5; matrix products, arithmetic and copies ran while one was open for 6% -> 7% of each run, Pallas kernels for 0% -> 0%
where the time goes in v1:
time: 514 us; the launch traced here: 511 us
  blocking collectives  199 us (39%)
  waiting for transfers between devices  196 us (38%)
  starting transfers between devices  38.4 us (7%)
  local copies, waits for them, and re-layouts  32.6 us (6%)
  matrix products  20.7 us (4%)
  between operations  14.6 us (3%)
  other arithmetic  10.5 us (2%)
    all_to_all x2, blocking collectives, inverse_transform(): lax.all_to_all(twisted, 'ctx', split_axis=3, concat_axis=2, tiled=True)  162 us
    all_to_all x2, waiting for transfers between devices, forward_transform(): lax.all_to_all(packed, 'ctx', split_axis=2, concat_axis=3, tiled=True)  131 us
    all_to_all x2, waiting for transfers between devices, forward_transform(): lax.all_to_all(signals, 'ctx', split_axis=2, concat_axis=1, tiled=True)  44.6 us
    all_to_all x1, blocking collectives, inverse_transform(): lax.all_to_all(spread, 'ctx', split_axis=1, concat_axis=2, tiled=True)  36.5 us
    all_to_all x2, starting transfers between devices, forward_transform(): lax.all_to_all(signals, 'ctx', split_axis=2, concat_axis=1, tiled=True)  20.9 us
    all_to_all x1, waiting for transfers between devices, inverse_transform(): lax.all_to_all(spread, 'ctx', split_axis=1, concat_axis=2, tiled=True)  19.7 us
    all_to_all x2, starting transfers between devices, forward_transform(): lax.all_to_all(packed, 'ctx', split_axis=2, concat_axis=3, tiled=True)  11.2 us
  transfers between devices with their start and end apart: 6, of which 5 were waited for; matrix products, arithmetic and copies ran while one was open for 7% of the time, Pallas kernels for 0%

profile of v1, /device:TPU:1, one launch (start us, length us, event | category | flops | bytes accessed | tf_op | source)
XLA Modules:
  0.0 511.1 jit_solution(9221389553091216282)
XLA Ops:
  7.2 1.6 fusion.64
  8.9 0.9 copy.209
  9.8 17.0 %all-to-all-start.4 = ((bf16[1,4,64,512]{3,1,0,2:T(4,128)(2,1)}), bf16[1,4,64,512]{3,1,0,2:T(4,128)(2,1)S(1)}, u32[]{:S(2)}, u32[]{:S(2)}) async-start(bf16[1,4,64,512]{3,1,0,2:T(4,128)(2,1)} %copy.209), calls=%async_computation.4 | async-start | bytes 524288 | tf_op jit(solution)/shard_map/all_to_all | solution.py:44
  27.6 1.2 copy.191
  28.8 18.5 %all-to-all-done.4 = bf16[1,4,64,512]{3,1,0,2:T(4,128)(2,1)S(1)} async-done(((bf16[1,4,64,512]{3,1,0,2:T(4,128)(2,1)}), bf16[1,4,64,512]{3,1,0,2:T(4,128)(2,1)S(1)}, u32[]{:S(2)}, u32[]{:S(2)}) %all-to-all-start.4) | async-done | bytes 262176 | tf_op jit(solution)/shard_map/all_to_all | solution.py:44
  47.3 3.9 all-to-all-start
  51.8 0.8 convolution_bitcast_fusion
  52.6 0.9 fusion.51
  53.6 2.1 copy.213
  55.7 26.1 %all-to-all-done = bf16[2,4,64,512]{3,1,0,2:T(4,128)(2,1)S(1)} async-done(((bf16[2,4,64,512]{3,1,0,2:T(4,128)(2,1)}), bf16[2,4,64,512]{3,1,0,2:T(4,128)(2,1)S(1)}, u32[]{:S(2)}, u32[]{:S(2)}) %all-to-all-start) | async-done | bytes 524320 | tf_op jit(solution)/shard_map/all_to_all | solution.py:44
  81.8 4.6 all-to-all-start.5
  87.3 0.9 fusion.82
  88.2 1.1 fusion.39
  89.6 4.1 copy.196
  93.7 44.4 %all-to-all-done.5 = bf16[2,1,256,2,512]{4,3,1,0,2:T(2,128)(2,1)S(1)} async-done(((bf16[2,1,256,2,512]{4,3,1,0,2:T(2,128)(2,1)}), bf16[2,1,256,2,512]{4,3,1,0,2:T(2,128)(2,1)S(1)}, u32[]{:S(2)}, u32[]{:S(2)}) %all-to-all-start.5) | async-done | bytes 1048608 | tf_op jit(solution)/shard_map/all_to_all | solution.py:49
  138.1 6.6 %all-to-all-start.1 = ((bf16[2,2,256,2,512]{4,3,1,0,2:T(2,128)(2,1)}), bf16[2,2,256,2,512]{4,3,1,0,2:T(2,128)(2,1)S(1)}, u32[]{:S(2)}, u32[]{:S(2)}) async-start(bf16[2,2,256,2,512]{4,3,1,0,2:T(2,128)(2,1)} %copy.196), calls=%async_computation.1 | async-start | bytes 4194304 | tf_op jit(solution)/shard_map/all_to_all | solution.py:49
  145.3 0.9 fusion.228
  146.9 2.4 copy.216
  149.3 1.2 reshape.609
  150.9 1.4 fusion.18
  152.3 1.4 fusion.103
  153.7 86.8 %all-to-all-done.1 = bf16[2,2,256,2,512]{4,3,1,0,2:T(2,128)(2,1)S(1)} async-done(((bf16[2,2,256,2,512]{4,3,1,0,2:T(2,128)(2,1)}), bf16[2,2,256,2,512]{4,3,1,0,2:T(2,128)(2,1)S(1)}, u32[]{:S(2)}, u32[]{:S(2)}) %all-to-all-start.1) | async-done | bytes 2097184 | tf_op jit(solution)/shard_map/all_to_all | solution.py:49
  241.2 1.2 fusion.227
  242.5 1.1 copy.198
  244.0 1.9 fusion.111
  247.1 2.1 copy.199
  249.3 1.5 squeeze.13
  250.7 2.1 fusion.9
  254.6 1.1 fusion.33
  257.5 0.9 fusion.41
  258.6 1.2 copy.217
  259.8 104.9 %all_to_all.117 = bf16[2,2,8,64,512]{4,2,1,0,3:T(8,128)(2,1)S(1)} all-to-all(bf16[2,2,8,64,512]{4,2,1,0,3:T(8,128)(2,1)S(1)} %copy.217), channel_id=1, replica_groups=mesh['dp'=16,'ctx'=32] {'ctx'}, dimensions={3} | all-to-all | bytes 4194304 | tf_op jit(solution)/shard_map/all_to_all | solution.py:81
  365.1 0.9 fusion.43
  366.1 1.0 fusion.22
  367.6 36.5 %all_to_all.118 = bf16[2,128,2,512]{3,2,0,1:T(2,128)(2,1)S(1)} all-to-all(bf16[2,128,2,512]{3,2,0,1:T(2,128)(2,1)S(1)} %copy.223), channel_id=1, replica_groups=mesh['dp'=16,'ctx'=32] {'ctx'}, dimensions={1} | all-to-all | bytes 1048576 | tf_op jit(solution)/shard_map/all_to_all | solution.py:86
  404.7 0.8 all_gather.6
  408.0 57.3 %all_to_all.119 = bf16[2,1,8,64,512]{4,2,1,0,3:T(8,128)(2,1)S(1)} all-to-all(bf16[2,1,8,64,512]{4,2,1,0,3:T(8,128)(2,1)S(1)} %copy.200), channel_id=1, replica_groups=mesh['dp'=16,'ctx'=32] {'ctx'}, dimensions={3} | all-to-all | bytes 2097152 | tf_op jit(solution)/shard_map/all_to_all | solution.py:81
  465.4 0.8 fusion.61
  466.2 0.8 fusion.25
  467.0 0.9 copy.206
  467.9 6.1 %all-to-all-start.3 = ((bf16[1,128,2,512]{3,2,0,1:T(2,128)(2,1)}), bf16[1,128,2,512]{3,2,0,1:T(2,128)(2,1)S(1)}, u32[]{:S(2)}, u32[]{:S(2)}) async-start(bf16[1,128,2,512]{3,2,0,1:T(2,128)(2,1)} %copy.206), calls=%async_computation.3 | async-start | bytes 524288 | tf_op jit(solution)/shard_map/all_to_all | solution.py:86
  474.2 19.7 %all-to-all-done.3 = bf16[1,128,2,512]{3,2,0,1:T(2,128)(2,1)S(1)} async-done(((bf16[1,128,2,512]{3,2,0,1:T(2,128)(2,1)}), bf16[1,128,2,512]{3,2,0,1:T(2,128)(2,1)S(1)}, u32[]{:S(2)}, u32[]{:S(2)}) %all-to-all-start.3) | async-done | bytes 262176 | tf_op jit(solution)/shard_map/all_to_all | solution.py:86
  495.3 0.7 copy.228
  496.6 2.6 fusion.58
  499.2 0.7 copy.229
  499.9 0.7 copy.230
  500.7 2.8 reduce_sum.12
  503.5 0.7 multiply_convert_fusion
  (74 shorter events, 16.5 us)
Async XLA Ops:
  7.2 19.6 %copy-start.6 = (bf16[1,256,512]{2,1,0:T(8,128)(2,1)S(1)}, bf16[1,256,512]{2,1,0:T(8,128)(2,1)}, u32[]{:S(2)}) copy-start(bf16[1,256,512]{2,1,0:T(8,128)(2,1)} %param.7) | copy-start | bytes 786436
  7.2 19.6 %copy-start.7 = (bf16[1,256,512]{2,1,0:T(8,128)(2,1)S(1)}, bf16[1,256,512]{2,1,0:T(8,128)(2,1)}, u32[]{:S(2)}) copy-start(bf16[1,256,512]{2,1,0:T(8,128)(2,1)} %param.8) | copy-start | bytes 786436
  8.8 18.6 %copy-start.10 = (s32[1,4]{1,0:T(1,128)S(1)}, s32[1,4]{1,0:T(1,128)}, u32[]{:S(2)}) copy-start(s32[1,4]{1,0:T(1,128)} %param.11) | copy-start | bytes 52
  8.9 18.6 %copy-start.9 = (bf16[256,512]{1,0:T(8,128)(2,1)S(1)}, bf16[256,512]{1,0:T(8,128)(2,1)}, u32[]{:S(2)}) copy-start(bf16[256,512]{1,0:T(8,128)(2,1)} %param.9) | copy-start | bytes 786436
  9.8 37.5 %all-to-all-start.4 = ((bf16[1,4,64,512]{3,1,0,2:T(4,128)(2,1)}), bf16[1,4,64,512]{3,1,0,2:T(4,128)(2,1)S(1)}, u32[]{:S(2)}, u32[]{:S(2)}) async-start(bf16[1,4,64,512]{3,1,0,2:T(4,128)(2,1)} %copy.209), calls=%async_computation.4 | async-start | bytes 524288 | tf_op jit(solution)/shard_map/all_to_all | solution.py:44
  47.3 34.5 %all-to-all-start = ((bf16[2,4,64,512]{3,1,0,2:T(4,128)(2,1)}), bf16[2,4,64,512]{3,1,0,2:T(4,128)(2,1)S(1)}, u32[]{:S(2)}, u32[]{:S(2)}) async-start(bf16[2,4,64,512]{3,1,0,2:T(4,128)(2,1)} %copy.191), calls=%async_computation | async-start | bytes 1048576 | tf_op jit(solution)/shard_map/all_to_all | solution.py:44
  81.8 56.3 %all-to-all-start.5 = ((bf16[2,1,256,2,512]{4,3,1,0,2:T(2,128)(2,1)}), bf16[2,1,256,2,512]{4,3,1,0,2:T(2,128)(2,1)S(1)}, u32[]{:S(2)}, u32[]{:S(2)}) async-start(bf16[2,1,256,2,512]{4,3,1,0,2:T(2,128)(2,1)} %copy.213), calls=%async_computation.5 | async-start | bytes 2097152 | tf_op jit(solution)/shard_map/all_to_all | solution.py:49
  138.1 102.5 %all-to-all-start.1 = ((bf16[2,2,256,2,512]{4,3,1,0,2:T(2,128)(2,1)}), bf16[2,2,256,2,512]{4,3,1,0,2:T(2,128)(2,1)S(1)}, u32[]{:S(2)}, u32[]{:S(2)}) async-start(bf16[2,2,256,2,512]{4,3,1,0,2:T(2,128)(2,1)} %copy.196), calls=%async_computation.1 | async-start | bytes 4194304 | tf_op jit(solution)/shard_map/all_to_all | solution.py:49
  144.7 356.0 %all-gather.2.cloned.1.call-start = ((), (), s32[]{:S(2)}) async-start(), calls=%async_computation.8 | async-start | bytes 4456448 | tf_op jit(solution)/shard_map/all_gather | solution.py:147
  150.5 1.8 copy-start.1
  245.9 1.2 copy-start
  252.9 1.0 copy-start.2
  252.9 1.4 copy-start.3
  252.9 1.7 copy-start.4
  466.2 28.5 %copy-start.5 = (bf16[1,256,512]{2,1,0:T(8,128)(2,1)S(1)}, bf16[1,256,512]{2,1,0:T(8,128)(2,1)}, u32[]{:S(2)}) copy-start(bf16[1,256,512]{2,1,0:T(8,128)(2,1)} %param.10) | copy-start | bytes 786436
  467.9 25.9 %all-to-all-start.3 = ((bf16[1,128,2,512]{3,2,0,1:T(2,128)(2,1)}), bf16[1,128,2,512]{3,2,0,1:T(2,128)(2,1)S(1)}, u32[]{:S(2)}, u32[]{:S(2)}) async-start(bf16[1,128,2,512]{3,2,0,1:T(2,128)(2,1)} %copy.206), calls=%async_computation.3 | async-start | bytes 524288 | tf_op jit(solution)/shard_map/all_to_all | solution.py:86
  494.1 2.4 copy-start.8
Sparse Core Ops, SparseCore 0:
  405.7 69.6 all-gather.1
